TPU v7x, 256 devices: a whole 4x4x8 slice. The times are simulated.
256 devices in a mesh: row: 16 (over y, x_lo, core), col: 16 (over x_hi, z).
Axes of the slice: x: 4 (x_hi: 2, x_lo: 2; x = x_hi * 2 + x_lo), y: 4, z: 8, core: 2. Of those that a mesh axis runs over, the one named last changes fastest.
Arguments:
- tokens: bfloat16 [1536, 8192], P('col', 'row'), may hold values from -6 to 6
- gate_weight: bfloat16 [8192, 29568], P('row', 'col'), may hold values from -0.0625 to 0.0625
- up_weight: bfloat16 [8192, 29568], P('row', 'col'), may hold values from -0.0625 to 0.0625
- gate_lower: bfloat16 [16, 8192, 64], P('col', 'row'), may hold values from -0.0625 to 0.0625
- up_lower: bfloat16 [16, 8192, 64], P('col', 'row'), may hold values from -0.0625 to 0.0625
- gate_upper: bfloat16 [16, 64, 29568], P('row', None, 'col'), may hold values from -0.21875 to 0.21875
- up_upper: bfloat16 [16, 64, 29568], P('row', None, 'col'), may hold values from -0.21875 to 0.21875
- outgoing: int32 [1], replicated, may hold values from 0 to 15
- incoming: int32 [1], replicated, may hold values from 0 to 15
Outputs:
- new_gate: bfloat16 [8192, 29568], P('row', 'col')
- new_up: bfloat16 [8192, 29568], P('row', 'col')
- hidden: bfloat16 [1536, 29568], P('row', 'col')
All inputs are finite; a program needn't handle non-finite values.
Results may differ from a plain program's by a relative error of at most 0.0058.
Values may be sent and summed in bfloat16 or wider, within the bound.
A program may use at most 128 MiB of HBM per device.

v0:
```python
import jax
import jax.numpy as jnp
from jax import lax
from jax.sharding import PartitionSpec as P


def broadcast(value, axis, root):
    mine = lax.axis_index(axis) == root
    return lax.psum(jnp.where(mine, value, jnp.zeros_like(value)), axis)


def lower_slot(stacked, ident):
    local = stacked.shape[1]
    chosen = lax.dynamic_index_in_dim(stacked, ident % local, 1, keepdims=False)
    return broadcast(chosen, "col", ident // local)


def upper_slot(stacked, ident):
    local = stacked.shape[1]
    chosen = lax.dynamic_index_in_dim(stacked, ident % local, 1, keepdims=False)
    return broadcast(chosen, "row", ident // local)


def merged(weight, low_old, low_new, up_old, up_new):
    delta = jnp.dot(low_new, up_new, preferred_element_type=jnp.float32) - jnp.dot(
        low_old, up_old, preferred_element_type=jnp.float32
    )
    return (weight.astype(jnp.float32) + delta).astype(jnp.bfloat16)


def body(
    tokens, gate_weight, up_weight, gate_lower, up_lower, gate_upper, up_upper, outgoing, incoming
):
    old = outgoing[0]
    new = incoming[0]
    lower_stack = jnp.stack([gate_lower, up_lower])
    upper_stack = jnp.stack([gate_upper, up_upper])
    lower_old = lower_slot(lower_stack, old)
    lower_new = lower_slot(lower_stack, new)
    upper_old = upper_slot(upper_stack, old)
    upper_new = upper_slot(upper_stack, new)
    new_gate = merged(gate_weight, lower_old[0], lower_new[0], upper_old[0], upper_new[0])
    new_up = merged(up_weight, lower_old[1], lower_new[1], upper_old[1], upper_new[1])
    gathered = lax.all_gather(tokens, "col", axis=0, tiled=True)
    width = new_gate.shape[1]
    gate_part = jnp.dot(gathered, new_gate, preferred_element_type=jnp.float32)
    up_part = jnp.dot(gathered, new_up, preferred_element_type=jnp.float32)
    summed = lax.psum_scatter(
        jnp.concatenate([gate_part, up_part], axis=1), "row", scatter_dimension=0, tiled=True
    )
    gate_sum = summed[:, :width]
    up_sum = summed[:, width:]
    hidden = (jax.nn.silu(gate_sum) * up_sum).astype(jnp.bfloat16)
    return (new_gate, new_up, hidden)


def solution(mesh):
    return jax.shard_map(
        body,
        mesh=mesh,
        in_specs=(
            P("col", "row"),
            P("row", "col"),
            P("row", "col"),
            P("col", "row", None),
            P("col", "row", None),
            P("row", None, "col"),
            P("row", None, "col"),
            P(),
            P(),
        ),
        out_specs=(P("row", "col"), P("row", "col"), P("row", "col")),
        check_vma=False,
    )
```

profile of v0, /device:TPU:16, one launch (start us, length us, event | category | flops | bytes accessed | tf_op | source)
XLA Modules:
  0.0 669.6 jit_solution(3130700918735361620)
XLA Ops:
  8.5 1.6 select_bitcast_fusion.2
  10.1 0.0 all-reduce.7.cloned.1.call-start
  10.2 2.1 select_bitcast_fusion
  12.4 0.7 all-gather.2.cloned.1.call-update
  13.1 156.5 %all-reduce.5.cloned.1.call-done = (bf16[2,512,64]{1,2,0:T(8,128)(2,1)}, bf16[2,512,64]{1,2,0:T(8,128)(2,1)}) async-done(((bf16[2,512,64]{1,2,0:T(8,128)(2,1)}, bf16[2,512,64]{1,2,0:T(8,128)(2,1)}), (bf16[2,512,64]{1,2,0:T(8,128)(2,1)}, bf16[2,512,64]{1,2,0:T(8,128)(2,1)})) %all-reduce.5.cloned.1.call-update) | async-done | bytes 262160 | tf_op jit(solution)/shard_map/psum | solution.py:9
  169.7 116.9 %all-reduce.7.cloned.1.call-done = (bf16[2,64,1848]{2,1,0:T(8,128)(2,1)}, bf16[2,64,1848]{2,1,0:T(8,128)(2,1)}) async-done(((bf16[2,64,1848]{2,1,0:T(8,128)(2,1)}, bf16[2,64,1848]{2,1,0:T(8,128)(2,1)}), (bf16[2,64,1848]{2,1,0:T(8,128)(2,1)}, bf16[2,64,1848]{2,1,0:T(8,128)(2,1)})) %all-reduce.7.cloned.1.call-update) | async-done | bytes 946192 | tf_op jit(solution)/shard_map/psum | solution.py:9
  286.5 1.7 fusion
  288.3 0.7 fusion.1
  289.0 0.8 copy-done
  289.8 0.1 copy-done.3
  289.9 0.7 add_convert_fusion
  290.6 0.8 copy-done.1
  291.4 2.0 add_convert_fusion.1
  293.5 85.0 %all-gather.2.cloned.1.call-done = bf16[1536,512]{1,0:T(8,128)(2,1)} async-done(((bf16[96,512]{1,0:T(8,128)(2,1)}), bf16[1536,512]{1,0:T(8,128)(2,1)}) %all-gather.2.cloned.1.call-update) | async-done | bytes 1572880 | tf_op jit(solution)/shard_map/all_gather | solution.py:44
  378.5 5.2 convolution_bitcast_fusion.1
  383.8 3.1 convolution_bitcast_fusion
  386.9 8.7 %pad_maximum_fusion = f32[1536,3696]{0,1:T(8,128)} fusion(f32[1536,1848]{0,1:T(8,128)S(1)} %convolution_bitcast_fusion, f32[1536,1848]{0,1:T(8,128)S(1)} %convolution_bitcast_fusion.1), kind=kLoop, calls=%fused_computation | loop fusion | flops 5677056 | bytes 45416448 | tf_op jit(solution)/shard_map/concatenate | solution.py:49
  395.6 23.5 %copy.14 = f32[1536,3696]{1,0:T(8,128)} copy(f32[1536,3696]{0,1:T(8,128)} %pad_maximum_fusion) | data formatting | bytes 45416448
  419.1 240.4 %reduce-scatter.4.cloned.1.call-done = f32[96,3696]{1,0:T(8,128)} async-done(((f32[1536,3696]{1,0:T(8,128)}), f32[96,3696]{1,0:T(8,128)}) %reduce-scatter.4.cloned.1.call-update) | async-done | bytes 1419280
  659.6 1.6 fusion.2
  661.2 0.3 copy.16
  661.5 0.3 copy.17
  661.8 0.3 multiply_convert_fusion
  662.1 0.9 copy.13
  (19 shorter events, 0.2 us)
Async XLA Ops:
  7.2 162.5 %all-reduce.5.cloned.1.call-start = ((), (), s32[]{:S(2)}) async-start(), calls=%async_computation.3 | async-start | bytes 524288 | tf_op jit(solution)/shard_map/psum | solution.py:9
  10.1 276.4 %all-reduce.7.cloned.1.call-start = ((), (), s32[]{:S(2)}) async-start(), calls=%async_computation.4 | async-start | bytes 1966080 | tf_op jit(solution)/shard_map/psum | solution.py:9
  12.3 366.2 %all-gather.2.cloned.1.call-start = ((), (), s32[]{:S(2)}) async-start(), calls=%async_computation.1 | async-start | bytes 1671168 | tf_op jit(solution)/shard_map/all_gather | solution.py:44
  13.1 646.5 %reduce-scatter.4.cloned.1.call-start = ((), (), s32[]{:S(2)}) async-start(), calls=%async_computation.2 | async-start | bytes 24231936
  169.7 118.6 %copy-start.5 = (bf16[2,512,64]{1,2,0:T(8,128)(2,1)S(1)}, bf16[2,512,64]{1,2,0:T(8,128)(2,1)}, u32[]{:S(2)}) copy-start(bf16[2,512,64]{1,2,0:T(8,128)(2,1)} %get-tuple-element.9) | copy-start | bytes 393220
  286.5 1.7 copy-start.4
  288.3 1.5 copy-start
  288.3 1.6 copy-start.3
  288.3 1.6 copy-start.6
  289.9 1.5 copy-start.1
  291.4 92.3 %copy-start.2 = (bf16[512,1848]{0,1:T(8,128)(2,1)}, bf16[512,1848]{0,1:T(8,128)(2,1)S(1)}, u32[]{:S(2)}) copy-start(bf16[512,1848]{0,1:T(8,128)(2,1)S(1)} %add_convert_fusion) | copy-start | bytes 5677060
  378.5 5.3 copy-start.7
Sparse Core Ops, SparseCore 0:
  11.2 158.3 all-reduce.4
  173.2 113.3 all-reduce.6
  289.1 89.3 all-gather.1
  419.3 240.2 reduce-scatter.3
where the time goes:
time: 672 us; the launch traced here: 670 us
  waiting for transfers between devices  600 us (89%)
  local copies, waits for them, and re-layouts  28.4 us (4%)
  between operations  15.2 us (2%)
  matrix products  13.5 us (2%)
  other arithmetic  12.7 us (2%)
    psum x2, waiting for transfers between devices, broadcast(): return lax.psum(jnp.where(mine, value, jnp.zeros_like(value)), axis)  273 us
    unnamed x5, waiting for transfers between devices  241 us
    all_gather x1, waiting for transfers between devices, body(): gathered = lax.all_gather(tokens, 'col', axis=0, tiled=True)  85 us
    unnamed x20, local copies, waits for them, and re-layouts  26.8 us
  transfers between devices with their start and end apart: 4, of which 4 were waited for; matrix products, arithmetic and copies ran while one was open for 1% of the time, Pallas kernels for 0%

commit v1 on v0

v1 whole, which is shorter than its diff:
```python
import jax
import jax.numpy as jnp
from jax import lax
from jax.experimental import pallas as pl
from jax.experimental.pallas import tpu as pltpu
from jax.sharding import PartitionSpec as P

MESH = pl.DeviceIdType.MESH
BF, F32 = jnp.bfloat16, jnp.float32
ROWS, DEPTH, FF, RANK = 96, 512, 1848, 64
WIDE, CHUNKS = 256, 7
MAIN = WIDE * CHUNKS
LAST = FF - MAIN
CROSS = (0, 2, 4)
ALONG = (1, 3, 5, 6)


class Semaphores:
    def __init__(self):
        self.names = {}

    def of(self, *name):
        return self.names.setdefault(name, len(self.names))


def kernel(
    tok, gw, uw, gl, ul, gu, uu, out_s, inc_s,
    ng, nu, hid,
    T, wg, wu, vg, vu, wc, wt, pad, lc, lr, lf, uc, u0, us, ur, uf,
    part, parts_last, rx, qo, qa, ro, ra, acc, fs, fx, to, ta, tacc, ts, tx,
    ssem, rsem, lsem,
):
    row, col = lax.axis_index("row"), lax.axis_index("col")
    k, chip = row % 2, row // 2
    y, xm = row // 4, (row // 2) % 2
    xo = 1 - xm
    yp, yo, ym = (y + 1) % 4, (y + 2) % 4, (y + 3) % 4
    xh, z = col // 8, col % 8
    names = Semaphores()

    partner = (chip * 2 + 1 - k, col)
    cross = (y * 4 + xo * 2 + k, col)
    up_y = (yp * 4 + xm * 2 + k, col)
    down_y = (ym * 4 + xm * 2 + k, col)
    far_x = (row, (1 - xh) * 8 + z)
    up_z = (row, xh * 8 + (z + 1) % 8)
    down_z = (row, xh * 8 + (z + 7) % 8)

    def copy(src, dst, target, index):
        return pltpu.make_async_remote_copy(
            src_ref=src, dst_ref=dst, send_sem=ssem.at[index], recv_sem=rsem.at[index],
            device_id=target, device_id_type=MESH,
        )

    sent = []

    def send(src, dst, target, *name):
        c = copy(src, dst, target, names.of(*name))
        c.start()
        sent.append(c)
        return c

    load_g = pltpu.make_async_copy(gw, wg, lsem.at[0])
    load_u = pltpu.make_async_copy(uw, wu, lsem.at[1])
    load_g.start()
    load_u.start()

    new, old = inc_s[0], out_s[0]
    zero = jnp.zeros((), BF)
    for m, ref in enumerate((gu, uu)):
        b = ref[0]
        uc[m, 0:4] = jnp.where(new == row, b, jnp.zeros_like(b)).reshape(4, 16, FF)
        uc[m, 4:8] = jnp.where(old == row, -b, jnp.zeros_like(b)).reshape(4, 16, FF)
    for m, ref in enumerate((gl, ul)):
        a = ref[0]
        both = jnp.concatenate(
            [jnp.where(new == col, a, jnp.zeros_like(a)), jnp.where(old == col, a, jnp.zeros_like(a))], axis=1
        )
        lc[:, m] = both.reshape(16, 32, 128)

    barrier = pltpu.get_barrier_semaphore()
    pl.semaphore_signal(barrier, inc=1, device_id=partner, device_id_type=MESH)
    for i in range(1, 8):
        pl.semaphore_signal(barrier, inc=1, device_id=((chip + i) % 8 * 2 + k, col), device_id_type=MESH)
    for i in range(1, 16):
        pl.semaphore_signal(barrier, inc=1, device_id=(row, (col + i) % 16), device_id_type=MESH)
    pl.semaphore_wait(barrier, 23)

    even = k == z % 2
    xs, ys = (z // 2) % 2, col // 4
    t0 = copy(tok, T.at[xs, ys, :, DEPTH:], partner, names.of("t0"))

    @pl.when(jnp.logical_not(even))
    def _():
        t0.start()

    @pl.when(even)
    def _():
        T[xs, ys, :, 0:DEPTH] = tok[...]

    c_u0 = send(uc.at[1 - k], u0, partner, "u0")
    l1 = [send(lc.at[(col + i) % 16], lr.at[i - 1], (row, (col + i) % 16), "l1", i) for i in range(1, 16)]

    def block(zz, q):
        return T.at[(zz // 2) % 2, (xh + q) % 2 * 2 + zz // 4]

    def hop(direction, stage, q, zz):
        target = (up_z, down_z)[direction]
        return copy(block(zz, q), block(zz, q), target, names.of("z", direction, stage, q))

    def source(direction, distance):
        return (z - distance + 8) % 8 if direction == 0 else (z + distance) % 8

    far = copy(block(z, 0), block(z, 0), far_x, names.of("h"))
    far_in = copy(block(z, 1), block(z, 1), far_x, names.of("h"))

    @pl.when(even)
    def _():
        t0.wait_recv()
        far.start()
        for d in range(2):
            hop(d, 1, 0, z).start()

    c_u0.wait_recv()
    us[...] = uc[k] + u0[...]
    u1 = [send(us.at[(chip + i) % 8], ur.at[i - 1], ((chip + i) % 8 * 2 + k, col), "u1", i) for i in range(1, 8)]

    @pl.when(even)
    def _():
        far_in.wait_recv()
        for d in range(2):
            hop(d, 1, 1, z).start()

    @pl.when(jnp.logical_not(even))
    def _():
        for q in range(2):
            for d in range(2):
                hop(d, 1, q, source(d, 1)).wait_recv()
                hop(d, 2, q, source(d, 1)).start()

    for c in u1:
        c.wait_recv()
    total = us[chip].astype(F32)
    for i in range(7):
        total = total + ur[i].astype(F32)
    uf[k, chip] = total.astype(BF)
    u2 = [send(uf.at[k, chip], uf.at[k, chip], ((chip + i) % 8 * 2 + k, col), "u2", i) for i in range(1, 8)]
    u3 = [send(uf.at[k, chip], uf.at[k, chip], partner, "u3", 0)]

    for c in l1:
        c.wait_recv()
    total = lc[col].astype(F32)
    for i in range(15):
        total = total + lr[i].astype(F32)
    lf[col] = total.astype(BF)
    l2 = [send(lf.at[col], lf.at[col], (row, (col + i) % 16), "l2", i) for i in range(1, 16)]

    @pl.when(even)
    def _():
        for q in range(2):
            for d in range(2):
                hop(d, 2, q, source(d, 2)).wait_recv()
                hop(d, 3, q, source(d, 2)).start()

    for i in range(1, 8):
        u2[i - 1].wait_recv()
        s = (chip - i + 8) % 8
        u3.append(send(uf.at[k, s], uf.at[k, s], partner, "u3", i))

    @pl.when(jnp.logical_not(even))
    def _():
        for q in range(2):
            for d in range(2):
                hop(d, 3, q, source(d, 3)).wait_recv()
                if d == q:
                    hop(d, 4, q, source(d, 3)).start()

    for c in l2:
        c.wait_recv()
    for c in u3:
        c.wait_recv()
    load_g.wait()
    load_u.wait()

    def swap(j):
        return copy(wc.at[j, :, 0:DEPTH], wc.at[j, :, DEPTH:], partner, first_swap + j)

    for j in range(CHUNKS):
        index = names.of("w", j)
        if j == 0:
            first_swap = index

    def merge(j, carry):
        cols = pl.ds(pl.multiple_of(j * WIDE, WIDE), WIDE)
        for m, (w, v) in enumerate(((wg, vg), (wu, vu))):
            delta = jnp.dot(
                lf[:, m].reshape(DEPTH, 2 * RANK), uf[m, :, :, cols].reshape(2 * RANK, WIDE),
                preferred_element_type=F32,
            )
            merged = (w[:, cols].astype(F32) + delta).astype(BF)
            v[:, cols] = merged
            wc[j, m, 0:DEPTH] = merged
        swap(j).start()
        return carry

    lax.fori_loop(0, CHUNKS, merge, 0)
    pad[...] = jnp.zeros_like(pad)
    for m, (w, v) in enumerate(((wg, vg), (wu, vu))):
        delta = jnp.dot(
            lf[:, m].reshape(DEPTH, 2 * RANK), uf[m, :, :, MAIN:FF].reshape(2 * RANK, LAST),
            preferred_element_type=F32,
        )
        merged = (w[:, MAIN:FF].astype(F32) + delta).astype(BF)
        v[:, MAIN:FF] = merged
        pad[m, :, 0:LAST] = merged.astype(F32)
    wt[0:DEPTH] = (pad[0] + pltpu.roll(pad[1], 64, 1)).astype(BF)
    c_wt = send(wt.at[0:DEPTH], wt.at[DEPTH:], partner, "wt")
    store_g = pltpu.make_async_copy(vg, ng, lsem.at[2])
    store_u = pltpu.make_async_copy(vu, nu, lsem.at[3])
    store_g.start()
    store_u.start()

    @pl.when(even)
    def _():
        hop(0, 4, 0, source(0, 4)).wait_recv()
        hop(1, 4, 1, source(1, 4)).wait_recv()

    def compute(j):
        swap(j).wait_recv()

        def quarter(i, carry):
            m, x = i // 2, i % 2
            p = jnp.dot(T[x].reshape(4 * ROWS, 2 * DEPTH), wc[j, m], preferred_element_type=F32)
            part[j, m, x] = p.astype(BF).reshape(4, ROWS, WIDE)
            return carry

        lax.fori_loop(0, 4, quarter, 0)

    def compute_last():
        c_wt.wait_recv()
        for x in range(2):
            p = jnp.dot(T[x].reshape(4 * ROWS, 2 * DEPTH), wt[...], preferred_element_type=F32)
            parts_last[x] = p.astype(BF).reshape(4, ROWS, 128)

    def add(ref, other):
        ref[...] = (ref[...].astype(F32) + other[...].astype(F32)).astype(BF)

    def finish(j, gate, up):
        h = gate / (1 + jnp.exp(-gate)) * up
        hid[:, j * WIDE:(j + 1) * WIDE] = h.astype(BF)

    ways = (up_y, down_y)
    near = (yp, ym)

    class Along:
        def __init__(self, i, j):
            self.i, self.j = i, j

        def start(self):
            i, j = self.i, self.j
            self.opposite = [send(part.at[j, d, :, yo], ro.at[i, d], ways[d], "ro", i, d) for d in range(2)]
            self.arrive = [send(part.at[j, 1 - d, :, near[d]], ra.at[i, d, 1 - d], ways[d], "ra", i, d, 1 - d) for d in range(2)]

        def forward(self):
            i, j = self.i, self.j
            for d in range(2):
                self.opposite[d].wait_recv()
                add(part.at[j, d, :, near[d]], ro.at[i, d])
                self.arrive.append(send(part.at[j, d, :, near[d]], ra.at[i, d, d], ways[d], "ra", i, d, d))

        def gather(self):
            i, j = self.i, self.j
            for c in self.arrive:
                c.wait_recv()

            def total(m, x):
                return part[j, m, x, y].astype(F32) + ra[i, 0, m, x].astype(F32) + ra[i, 1, m, x].astype(F32)

            for m in range(2):
                fs[i, m] = total(m, xo).astype(BF)
            self.last = send(fs.at[i], fx.at[i], cross, "fx", i)
            for m in range(2):
                acc[i, m] = total(m, xm)

        def end(self):
            i, j = self.i, self.j
            self.last.wait_recv()
            finish(j, acc[i, 0] + fx[i, 0].astype(F32), acc[i, 1] + fx[i, 1].astype(F32))

    class Cross:
        def __init__(self, i, j):
            self.i, self.j = i, j

        def start(self):
            i, j = self.i, self.j
            self.first = send(part.at[j, :, xo], rx.at[i], cross, "rx", i)

        def turn(self):
            i, j = self.i, self.j
            self.first.wait_recv()
            for m in range(2):
                add(part.at[j, m, xm], rx.at[i, m])
            self.opposite = [send(part.at[j, d, xm, yo], qo.at[i, d], ways[d], "qo", i, d) for d in range(2)]
            self.arrive = [send(part.at[j, 1 - d, xm, near[d]], qa.at[i, d, 1 - d], ways[d], "qa", i, d, 1 - d) for d in range(2)]

        def forward(self):
            i, j = self.i, self.j
            for d in range(2):
                self.opposite[d].wait_recv()
                add(part.at[j, d, xm, near[d]], qo.at[i, d])
                self.arrive.append(send(part.at[j, d, xm, near[d]], qa.at[i, d, d], ways[d], "qa", i, d, d))

        def end(self):
            i, j = self.i, self.j
            for c in self.arrive:
                c.wait_recv()

            def total(m):
                return part[j, m, xm, y].astype(F32) + qa[i, 0, m].astype(F32) + qa[i, 1, m].astype(F32)

            finish(j, total(0), total(1))

    class Last:
        def start(self):
            self.opposite = [send(parts_last.at[d, yo], to.at[d], ways[d], "to", d) for d in range(2)]
            self.arrive = [send(parts_last.at[1 - d, near[d]], ta.at[d, 1 - d], ways[d], "ta", d, 1 - d) for d in range(2)]

        def forward(self):
            for d in range(2):
                self.opposite[d].wait_recv()
                add(parts_last.at[d, near[d]], to.at[d])
                self.arrive.append(send(parts_last.at[d, near[d]], ta.at[d, d], ways[d], "ta", d, d))

        def gather(self):
            for c in self.arrive:
                c.wait_recv()

            def total(x):
                return parts_last[x, y].astype(F32) + ta[0, x].astype(F32) + ta[1, x].astype(F32)

            ts[...] = total(xo).astype(BF)
            self.last = send(ts, tx, cross, "tx")
            tacc[...] = total(xm)

        def end(self):
            self.last.wait_recv()
            gate = tacc[...] + tx[...].astype(F32)
            up = pltpu.roll(gate, 64, 1)
            h = gate / (1 + jnp.exp(-gate)) * up
            hid[:, MAIN:FF] = h[:, 0:LAST].astype(BF)

    along = [Along(i, j) for i, j in enumerate(ALONG)]
    crossed = [Cross(i, j) for i, j in enumerate(CROSS)]
    last = Last()
    for j in range(CHUNKS):
        compute(j)
        (crossed[CROSS.index(j)] if j in CROSS else along[ALONG.index(j)]).start()
    compute_last()
    last.start()
    along[0].forward()
    along[1].forward()
    crossed[0].turn()
    along[2].forward()
    along[3].forward()
    last.forward()
    along[0].gather()
    crossed[0].forward()
    crossed[1].turn()
    along[1].gather()
    crossed[1].forward()
    along[2].gather()
    crossed[0].end()
    crossed[2].turn()
    along[3].gather()
    last.gather()
    crossed[2].forward()
    crossed[1].end()
    along[0].end()
    along[1].end()
    along[2].end()
    along[3].end()
    last.end()
    crossed[2].end()

    for c in sent:
        c.wait_send()
    for j in range(CHUNKS):
        swap(j).wait_send()

    @pl.when(even)
    def _():
        far.wait_send()
        for q in range(2):
            for d in range(2):
                hop(d, 1, q, z).wait_send()
                hop(d, 3, q, source(d, 2)).wait_send()

    @pl.when(jnp.logical_not(even))
    def _():
        t0.wait_send()
        for q in range(2):
            for d in range(2):
                hop(d, 2, q, source(d, 1)).wait_send()
                if d == q:
                    hop(d, 4, q, source(d, 3)).wait_send()

    store_g.wait()
    store_u.wait()
    assert len(names.names) <= COPIES, len(names.names)


COPIES = 160


def body(*args):
    vmem = pl.BlockSpec(memory_space=pltpu.VMEM)
    smem = pl.BlockSpec(memory_space=pltpu.SMEM)
    anywhere = pl.BlockSpec(memory_space=pl.ANY)
    n_a, n_c = len(ALONG), len(CROSS)

    def b(*shape):
        return pltpu.VMEM(shape, BF)

    def f(*shape):
        return pltpu.VMEM(shape, F32)

    scratch = [
        b(2, 4, ROWS, 2 * DEPTH),
        b(DEPTH, FF), b(DEPTH, FF), b(DEPTH, FF), b(DEPTH, FF),
        b(CHUNKS, 2, 2 * DEPTH, WIDE),
        b(2 * DEPTH, 128),
        f(2, DEPTH, 128),
        b(16, 2, 32, 128), b(15, 2, 32, 128), b(16, 2, 32, 128),
        b(2, 8, 16, FF), b(8, 16, FF), b(8, 16, FF), b(7, 16, FF), b(2, 8, 16, FF),
        b(CHUNKS, 2, 2, 4, ROWS, WIDE),
        b(2, 4, ROWS, 128),
        b(n_c, 2, 4, ROWS, WIDE), b(n_c, 2, ROWS, WIDE), b(n_c, 2, 2, ROWS, WIDE),
        b(n_a, 2, 2, ROWS, WIDE), b(n_a, 2, 2, 2, ROWS, WIDE),
        f(n_a, 2, ROWS, WIDE), b(n_a, 2, ROWS, WIDE), b(n_a, 2, ROWS, WIDE),
        b(2, ROWS, 128), b(2, 2, ROWS, 128), f(ROWS, 128), b(ROWS, 128), b(ROWS, 128),
        pltpu.SemaphoreType.DMA((COPIES,)), pltpu.SemaphoreType.DMA((COPIES,)), pltpu.SemaphoreType.DMA((4,)),
    ]
    return pl.pallas_call(
        kernel,
        out_shape=(
            jax.ShapeDtypeStruct((DEPTH, FF), BF),
            jax.ShapeDtypeStruct((DEPTH, FF), BF),
            jax.ShapeDtypeStruct((ROWS, FF), BF),
        ),
        in_specs=[vmem, anywhere, anywhere, vmem, vmem, vmem, vmem, smem, smem],
        out_specs=(anywhere, anywhere, vmem),
        scratch_shapes=scratch,
        compiler_params=pltpu.CompilerParams(
            collective_id=0, has_side_effects=True, vmem_limit_bytes=56 * 1024 * 1024
        ),
        cost_estimate=pl.CostEstimate(flops=7_000_000_000, bytes_accessed=10_000_000, transcendentals=200_000),
    )(*args)


def solution(mesh):
    return jax.shard_map(
        body,
        mesh=mesh,
        in_specs=(
            P("col", "row"),
            P("row", "col"),
            P("row", "col"),
            P("col", "row", None),
            P("col", "row", None),
            P("row", None, "col"),
            P("row", None, "col"),
            P(),
            P(),
        ),
        out_specs=(P("row", "col"), P("row", "col"), P("row", "col")),
        check_vma=False,
    )
```

time: 672 us -> 111 us (0.17)
  waiting for transfers between devices: 600 us -> 0 us
  Pallas kernels: 0 us -> 92.1 us
  matrix products: 13.5 us -> 0 us
  between operations: 15.2 us -> 1.94 us
  other arithmetic: 12.7 us -> 0 us
  local copies, waits for them, and re-layouts: 28.4 us -> 16.9 us
    psum x2 -> x0, waiting for transfers between devices: 273 us -> none  [broadcast(): return lax.psum(jnp.where(mine, value, jnp.zeros_like(value)), axis)]
    unnamed x5 -> x0, waiting for transfers between devices: 241 us -> none
    pallas_call x0 -> x1, Pallas kernels: none -> 92.1 us  [body(): pl.pallas_call(kernel, out_shape=(jax.ShapeDtypeStruct((DEPTH, FF), BF),...]
    all_gather x1 -> x0, waiting for transfers between devices: 85 us -> none  [body(): gathered = lax.all_gather(tokens, 'col', axis=0, tiled=True)]
    unnamed x20 -> x11, local copies, waits for them, and re-layouts: 26.8 us -> 10.5 us
    dot_general x6 -> x0, matrix products: 13.5 us -> none  [the longest x1 5.24 us: body(): gate_part = jnp.dot(gathered, new_gate, preferred_element_type=jnp.float32)]
    concatenate x1 -> x0, other arithmetic: 8.67 us -> none  [body(): jnp.concatenate([gate_part, up_part], axis=1)]
  transfers between devices with their start and end apart: 4 -> 0, of which waited for: 4 -> 0; matrix products, arithmetic and copies ran while one was open for 1% -> 0% of each run, Pallas kernels for 0% -> 0%
where the time goes in v1:
time: 111 us
  Pallas kernels  92.1 us (83%)
  local copies, waits for them, and re-layouts  16.9 us (15%)
  between operations  1.94 us (2%)
    pallas_call x1, Pallas kernels, body(): pl.pallas_call(kernel, out_shape=(jax.ShapeDtypeStruct((DEPTH, FF), BF),...  92.1 us
    unnamed x11, local copies, waits for them, and re-layouts  10.5 us
    pallas_call x2, local copies, waits for them, and re-layouts, body(): pl.pallas_call(kernel, out_shape=(jax.ShapeDtypeStruct((DEPTH, FF), BF),...  6.37 us

profile of v1, /device:TPU:16, one launch (start us, length us, event | category | flops | bytes accessed | tf_op | source)
XLA Modules:
  0.0 111.0 jit_solution(13063281667142654961)
XLA Ops:
  1.9 1.6 %copy.14.gl = bf16[1,512,64]{2,1,0:T(8,128)(2,1)} copy(bf16[1,512,64]{1,2,0:T(8,128)(2,1)} %param.12) | data formatting | bytes 131072 | tf_op args[3]
  3.5 1.6 %copy.15.ul = bf16[1,512,64]{2,1,0:T(8,128)(2,1)} copy(bf16[1,512,64]{1,2,0:T(8,128)(2,1)} %param.13) | data formatting | bytes 131072 | tf_op args[4]
  5.1 0.0 copy-start.1
  5.1 4.1 %copy.12.gw = bf16[512,1848]{1,0:T(8,128)(2,1)} copy(bf16[512,1848]{0,1:T(8,128)(2,1)} %param.10) | data formatting | bytes 3784704 | tf_op args[1]
  9.2 0.0 copy-done.1
  9.2 2.5 %copy.13.uw = bf16[512,1848]{1,0:T(8,128)(2,1)} copy(bf16[512,1848]{0,1:T(8,128)(2,1)S(1)} %copy-done.1) | data formatting | bytes 3784704 | tf_op args[2]
  11.7 92.1 %shard_map.112 = (bf16[512,1848]{1,0:T(8,128)(2,1)}, bf16[512,1848]{1,0:T(8,128)(2,1)}, bf16[96,1848]{1,0:T(8,128)(2,1)}) custom-call(bf16[96,512]{1,0:T(8,128)(2,1)} %tok.1, bf16[512,1848]{1,0:T(8,128)(2,1)} %copy.12.gw, bf16[512,1848]{1,0:T(8,128)(2,1)} %copy.13.uw, bf16[1,512,64]{2,1,0:T(8,128)(2,1)} %copy.14.gl, bf16[1,512,64]{2,1,0:T(8,128)(2,1)} %copy.15.ul, ...), custom_call_target="tpu_custom_call" | custom-call | flops 7000000000 | bytes 10000000 | tf_op jit(solution)/shard_map/pallas_call | solution.py:443
  103.9 0.0 copy-start
  103.9 4.1 %copy.16 = bf16[512,1848]{0,1:T(8,128)(2,1)} copy(bf16[512,1848]{1,0:T(8,128)(2,1)} %get-tuple-element.3) | data formatting | bytes 3784704 | tf_op jit(solution)/shard_map/pallas_call | solution.py:443
  108.0 0.0 copy-done
  108.0 0.0 copy-start.2
  108.0 2.3 %copy.17 = bf16[512,1848]{0,1:T(8,128)(2,1)} copy(bf16[512,1848]{1,0:T(8,128)(2,1)S(1)} %copy-done) | data formatting | bytes 3784704 | tf_op jit(solution)/shard_map/pallas_call | solution.py:443
  110.2 0.0 copy-done.2
  110.2 0.7 copy.21
Async XLA Ops:
  5.1 4.1 %copy-start.1 = (bf16[512,1848]{0,1:T(8,128)(2,1)S(1)}, bf16[512,1848]{0,1:T(8,128)(2,1)}, u32[]{:S(2)}) copy-start(bf16[512,1848]{0,1:T(8,128)(2,1)} %param.11) | copy-start | bytes 5677060
  103.9 4.1 %copy-start = (bf16[512,1848]{1,0:T(8,128)(2,1)S(1)}, bf16[512,1848]{1,0:T(8,128)(2,1)}, u32[]{:S(2)}) copy-start(bf16[512,1848]{1,0:T(8,128)(2,1)} %get-tuple-element.4) | copy-start | bytes 5677060
  108.0 2.3 %copy-start.2 = (bf16[96,1848]{1,0:T(8,128)(2,1)S(1)}, bf16[96,1848]{1,0:T(8,128)(2,1)}, u32[]{:S(2)}) copy-start(bf16[96,1848]{1,0:T(8,128)(2,1)} %get-tuple-element.11) | copy-start | bytes 1064452

commit v2 on v1

--- a/solution.py
+++ b/solution.py
@@ -25,8 +25,8 @@
 
 def kernel(
     tok, gw, uw, gl, ul, gu, uu, out_s, inc_s,
-    ng, nu, hid,
-    T, wg, wu, vg, vu, wc, wt, pad, lc, lr, lf, uc, u0, us, ur, uf,
+    vg, vu, hid,
+    T, wg, wu, wc, wt, lc, l0, ls, lr, lf, uc, u0, us, ur, uf,
     part, parts_last, rx, qo, qa, ro, ra, acc, fs, fx, to, ta, tacc, ts, tx,
     ssem, rsem, lsem,
 ):
@@ -65,78 +65,105 @@
     load_g.start()
     load_u.start()
 
+    barrier = pltpu.get_barrier_semaphore()
+    pl.semaphore_signal(barrier, inc=1, device_id=partner, device_id_type=MESH)
+    pl.semaphore_signal(barrier, inc=1, device_id=far_x, device_id_type=MESH)
+    for i in range(1, 8):
+        pl.semaphore_signal(barrier, inc=1, device_id=((chip + i) % 8 * 2 + k, col), device_id_type=MESH)
+        pl.semaphore_signal(barrier, inc=1, device_id=(row, xh * 8 + (z + i) % 8), device_id_type=MESH)
+
     new, old = inc_s[0], out_s[0]
-    zero = jnp.zeros((), BF)
     for m, ref in enumerate((gu, uu)):
         b = ref[0]
         uc[m, 0:4] = jnp.where(new == row, b, jnp.zeros_like(b)).reshape(4, 16, FF)
         uc[m, 4:8] = jnp.where(old == row, -b, jnp.zeros_like(b)).reshape(4, 16, FF)
     for m, ref in enumerate((gl, ul)):
         a = ref[0]
-        both = jnp.concatenate(
-            [jnp.where(new == col, a, jnp.zeros_like(a)), jnp.where(old == col, a, jnp.zeros_like(a))], axis=1
-        )
-        lc[:, m] = both.reshape(16, 32, 128)
-
-    barrier = pltpu.get_barrier_semaphore()
-    pl.semaphore_signal(barrier, inc=1, device_id=partner, device_id_type=MESH)
-    for i in range(1, 8):
-        pl.semaphore_signal(barrier, inc=1, device_id=((chip + i) % 8 * 2 + k, col), device_id_type=MESH)
-    for i in range(1, 16):
-        pl.semaphore_signal(barrier, inc=1, device_id=(row, (col + i) % 16), device_id_type=MESH)
-    pl.semaphore_wait(barrier, 23)
+        lc[8 * m:8 * m + 4] = jnp.where(new == col, a, jnp.zeros_like(a)).reshape(4, 16, DEPTH)
+        lc[8 * m + 4:8 * m + 8] = jnp.where(old == col, a, jnp.zeros_like(a)).reshape(4, 16, DEPTH)
+    pl.semaphore_wait(barrier, 16)
 
     even = k == z % 2
+    odd = jnp.logical_not(even)
     xs, ys = (z // 2) % 2, col // 4
-    t0 = copy(tok, T.at[xs, ys, :, DEPTH:], partner, names.of("t0"))
-
-    @pl.when(jnp.logical_not(even))
-    def _():
-        t0.start()
+    t0 = [
+        copy(tok.at[PART * p:PART * (p + 1)], T.at[xs, ys, PART * p:PART * (p + 1), DEPTH:], partner, names.of("t0", p))
+        for p in range(PARTS)
+    ]
+
+    @pl.when(odd)
+    def _():
+        for c in t0:
+            c.start()
 
     @pl.when(even)
     def _():
         T[xs, ys, :, 0:DEPTH] = tok[...]
 
+    c_l0 = send(lc.at[pl.ds(8 * (1 - xh), 8)], l0, far_x, "l0")
     c_u0 = send(uc.at[1 - k], u0, partner, "u0")
-    l1 = [send(lc.at[(col + i) % 16], lr.at[i - 1], (row, (col + i) % 16), "l1", i) for i in range(1, 16)]
-
-    def block(zz, q):
-        return T.at[(zz // 2) % 2, (xh + q) % 2 * 2 + zz // 4]
-
-    def hop(direction, stage, q, zz):
+
+    def block(zz, q, p):
+        return T.at[(zz // 2) % 2, (xh + q) % 2 * 2 + zz // 4, PART * p:PART * (p + 1)]
+
+    def hop(direction, stage, q, p, zz):
         target = (up_z, down_z)[direction]
-        return copy(block(zz, q), block(zz, q), target, names.of("z", direction, stage, q))
+        return copy(block(zz, q, p), block(zz, q, p), target, names.of("z", direction, stage, q, p))
 
     def source(direction, distance):
         return (z - distance + 8) % 8 if direction == 0 else (z + distance) % 8
 
-    far = copy(block(z, 0), block(z, 0), far_x, names.of("h"))
-    far_in = copy(block(z, 1), block(z, 1), far_x, names.of("h"))
+    def far(p, q):
+        return copy(block(z, q, p), block(z, q, p), far_x, names.of("h", p))
+
+    def forward(stage, q):
+        for p in range(PARTS):
+            for d in range(2):
+                hop(d, stage, q, p, source(d, stage)).wait_recv()
+                if stage < 3 or d == q:
+                    hop(d, stage + 1, q, p, source(d, stage)).start()
 
     @pl.when(even)
     def _():
-        t0.wait_recv()
-        far.start()
-        for d in range(2):
-            hop(d, 1, 0, z).start()
+        for p in range(PARTS):
+            t0[p].wait_recv()
+            for d in range(2):
+                hop(d, 1, 0, p, z).start()
+            far(p, 0).start()
 
     c_u0.wait_recv()
     us[...] = uc[k] + u0[...]
     u1 = [send(us.at[(chip + i) % 8], ur.at[i - 1], ((chip + i) % 8 * 2 + k, col), "u1", i) for i in range(1, 8)]
 
+    @pl.when(odd)
+    def _():
+        forward(1, 0)
+
+    c_l0.wait_recv()
+    ls[...] = lc[pl.ds(8 * xh, 8)] + l0[...]
+    l1 = [send(ls.at[(z + i) % 8], lr.at[i - 1], (row, xh * 8 + (z + i) % 8), "l1", i) for i in range(1, 8)]
+
     @pl.when(even)
     def _():
-        far_in.wait_recv()
-        for d in range(2):
-            hop(d, 1, 1, z).start()
-
-    @pl.when(jnp.logical_not(even))
-    def _():
-        for q in range(2):
-            for d in range(2):
-                hop(d, 1, q, source(d, 1)).wait_recv()
-                hop(d, 2, q, source(d, 1)).start()
+        for p in range(PARTS):
+            far(p, 1).wait_recv()
+            for d in range(2):
+                hop(d, 1, 1, p, z).start()
+        forward(2, 0)
+
+    @pl.when(odd)
+    def _():
+        forward(1, 1)
+
+    for c in l1:
+        c.wait_recv()
+    total = ls[z].astype(F32)
+    for i in range(7):
+        total = total + lr[i].astype(F32)
+    mine = col
+    lf[mine] = total.astype(BF)
+    l2 = [send(lf.at[mine], lf.at[mine], (row, xh * 8 + (z + i) % 8), "l2", i) for i in range(1, 8)]
+    l3 = [send(lf.at[mine], lf.at[mine], far_x, "l3", 0)]
 
     for c in u1:
         c.wait_recv()
@@ -147,35 +174,29 @@
     u2 = [send(uf.at[k, chip], uf.at[k, chip], ((chip + i) % 8 * 2 + k, col), "u2", i) for i in range(1, 8)]
     u3 = [send(uf.at[k, chip], uf.at[k, chip], partner, "u3", 0)]
 
-    for c in l1:
-        c.wait_recv()
-    total = lc[col].astype(F32)
-    for i in range(15):
-        total = total + lr[i].astype(F32)
-    lf[col] = total.astype(BF)
-    l2 = [send(lf.at[col], lf.at[col], (row, (col + i) % 16), "l2", i) for i in range(1, 16)]
+    @pl.when(odd)
+    def _():
+        forward(3, 0)
 
     @pl.when(even)
     def _():
-        for q in range(2):
-            for d in range(2):
-                hop(d, 2, q, source(d, 2)).wait_recv()
-                hop(d, 3, q, source(d, 2)).start()
+        forward(2, 1)
+
+    for i in range(1, 8):
+        l2[i - 1].wait_recv()
+        s = xh * 8 + (z - i + 8) % 8
+        l3.append(send(lf.at[s], lf.at[s], far_x, "l3", i))
+
+    @pl.when(odd)
+    def _():
+        forward(3, 1)
 
     for i in range(1, 8):
         u2[i - 1].wait_recv()
         s = (chip - i + 8) % 8
         u3.append(send(uf.at[k, s], uf.at[k, s], partner, "u3", i))
 
-    @pl.when(jnp.logical_not(even))
-    def _():
-        for q in range(2):
-            for d in range(2):
-                hop(d, 3, q, source(d, 3)).wait_recv()
-                if d == q:
-                    hop(d, 4, q, source(d, 3)).start()
-
-    for c in l2:
+    for c in l3:
         c.wait_recv()
     for c in u3:
         c.wait_recv()
@@ -183,54 +204,53 @@
     load_u.wait()
 
     def swap(j):
-        return copy(wc.at[j, :, 0:DEPTH], wc.at[j, :, DEPTH:], partner, first_swap + j)
+        return copy(wc.at[j, :, :, 0:DEPTH], wc.at[j, :, :, DEPTH:], partner, first_swap + j)
 
     for j in range(CHUNKS):
         index = names.of("w", j)
         if j == 0:
             first_swap = index
 
+    def merged(w, m, cols):
+        delta = lax.dot_general(
+            uf[m, :, :, cols].reshape(2 * RANK, -1), lf[8 * m:8 * m + 8].reshape(2 * RANK, DEPTH),
+            (((0,), (0,)), ((), ())), preferred_element_type=F32,
+        )
+        return (w[cols].astype(F32) + delta).astype(BF)
+
     def merge(j, carry):
         cols = pl.ds(pl.multiple_of(j * WIDE, WIDE), WIDE)
         for m, (w, v) in enumerate(((wg, vg), (wu, vu))):
-            delta = jnp.dot(
-                lf[:, m].reshape(DEPTH, 2 * RANK), uf[m, :, :, cols].reshape(2 * RANK, WIDE),
-                preferred_element_type=F32,
-            )
-            merged = (w[:, cols].astype(F32) + delta).astype(BF)
-            v[:, cols] = merged
-            wc[j, m, 0:DEPTH] = merged
+            piece = merged(w, m, cols)
+            v[cols] = piece
+            wc[j, m, :, 0:DEPTH] = piece
         swap(j).start()
         return carry
 
     lax.fori_loop(0, CHUNKS, merge, 0)
-    pad[...] = jnp.zeros_like(pad)
+    wt[:, 0:DEPTH] = jnp.zeros((128, DEPTH), BF)
     for m, (w, v) in enumerate(((wg, vg), (wu, vu))):
-        delta = jnp.dot(
-            lf[:, m].reshape(DEPTH, 2 * RANK), uf[m, :, :, MAIN:FF].reshape(2 * RANK, LAST),
-            preferred_element_type=F32,
+        piece = merged(w, m, slice(MAIN, FF))
+        v[MAIN:FF] = piece
+        wt[64 * m:64 * m + LAST, 0:DEPTH] = piece
+    c_wt = send(wt.at[:, 0:DEPTH], wt.at[:, DEPTH:], partner, "wt")
+    @pl.when(even)
+    def _():
+        for p in range(PARTS):
+            for d in range(2):
+                hop(d, 4, d, p, source(d, 4)).wait_recv()
+
+    def times(x, w):
+        return lax.dot_general(
+            T[x].reshape(4 * ROWS, 2 * DEPTH), w, (((1,), (1,)), ((), ())), preferred_element_type=F32
         )
-        merged = (w[:, MAIN:FF].astype(F32) + delta).astype(BF)
-        v[:, MAIN:FF] = merged
-        pad[m, :, 0:LAST] = merged.astype(F32)
-    wt[0:DEPTH] = (pad[0] + pltpu.roll(pad[1], 64, 1)).astype(BF)
-    c_wt = send(wt.at[0:DEPTH], wt.at[DEPTH:], partner, "wt")
-    store_g = pltpu.make_async_copy(vg, ng, lsem.at[2])
-    store_u = pltpu.make_async_copy(vu, nu, lsem.at[3])
-    store_g.start()
-    store_u.start()
-
-    @pl.when(even)
-    def _():
-        hop(0, 4, 0, source(0, 4)).wait_recv()
-        hop(1, 4, 1, source(1, 4)).wait_recv()
 
     def compute(j):
         swap(j).wait_recv()
 
         def quarter(i, carry):
             m, x = i // 2, i % 2
-            p = jnp.dot(T[x].reshape(4 * ROWS, 2 * DEPTH), wc[j, m], preferred_element_type=F32)
+            p = times(x, wc[j, m])
             part[j, m, x] = p.astype(BF).reshape(4, ROWS, WIDE)
             return carry
 
@@ -239,7 +259,7 @@
     def compute_last():
         c_wt.wait_recv()
         for x in range(2):
-            p = jnp.dot(T[x].reshape(4 * ROWS, 2 * DEPTH), wt[...], preferred_element_type=F32)
+            p = times(x, wt[...])
             parts_last[x] = p.astype(BF).reshape(4, ROWS, 128)
 
     def add(ref, other):
@@ -389,30 +409,35 @@
 
     @pl.when(even)
     def _():
-        far.wait_send()
-        for q in range(2):
-            for d in range(2):
-                hop(d, 1, q, z).wait_send()
-                hop(d, 3, q, source(d, 2)).wait_send()
-
-    @pl.when(jnp.logical_not(even))
-    def _():
-        t0.wait_send()
-        for q in range(2):
-            for d in range(2):
-                hop(d, 2, q, source(d, 1)).wait_send()
-                if d == q:
-                    hop(d, 4, q, source(d, 3)).wait_send()
-
-    store_g.wait()
-    store_u.wait()
+        for p in range(PARTS):
+            far(p, 0).wait_send()
+            for q in range(2):
+                for d in range(2):
+                    hop(d, 1, q, p, z).wait_send()
+                    hop(d, 3, q, p, source(d, 2)).wait_send()
+
+    @pl.when(odd)
+    def _():
+        for p in range(PARTS):
+            t0[p].wait_send()
+            for q in range(2):
+                for d in range(2):
+                    hop(d, 2, q, p, source(d, 1)).wait_send()
+                    if d == q:
+                        hop(d, 4, q, p, source(d, 3)).wait_send()
+
     assert len(names.names) <= COPIES, len(names.names)
 
 
-COPIES = 160
-
-
-def body(*args):
+COPIES = 192
+PARTS = 3
+PART = ROWS // PARTS
+
+
+def body(tokens, gate_weight, up_weight, gate_lower, up_lower, *others):
+    args = (
+        tokens, gate_weight.T, up_weight.T, gate_lower.swapaxes(1, 2), up_lower.swapaxes(1, 2), *others
+    )
     vmem = pl.BlockSpec(memory_space=pltpu.VMEM)
     smem = pl.BlockSpec(memory_space=pltpu.SMEM)
     anywhere = pl.BlockSpec(memory_space=pl.ANY)
@@ -426,11 +451,10 @@
 
     scratch = [
         b(2, 4, ROWS, 2 * DEPTH),
-        b(DEPTH, FF), b(DEPTH, FF), b(DEPTH, FF), b(DEPTH, FF),
-        b(CHUNKS, 2, 2 * DEPTH, WIDE),
-        b(2 * DEPTH, 128),
-        f(2, DEPTH, 128),
-        b(16, 2, 32, 128), b(15, 2, 32, 128), b(16, 2, 32, 128),
+        b(FF, DEPTH), b(FF, DEPTH),
+        b(CHUNKS, 2, WIDE, 2 * DEPTH),
+        b(128, 2 * DEPTH),
+        b(16, 16, DEPTH), b(8, 16, DEPTH), b(8, 16, DEPTH), b(7, 16, DEPTH), b(16, 16, DEPTH),
         b(2, 8, 16, FF), b(8, 16, FF), b(8, 16, FF), b(7, 16, FF), b(2, 8, 16, FF),
         b(CHUNKS, 2, 2, 4, ROWS, WIDE),
         b(2, 4, ROWS, 128),
@@ -440,21 +464,22 @@
         b(2, ROWS, 128), b(2, 2, ROWS, 128), f(ROWS, 128), b(ROWS, 128), b(ROWS, 128),
         pltpu.SemaphoreType.DMA((COPIES,)), pltpu.SemaphoreType.DMA((COPIES,)), pltpu.SemaphoreType.DMA((4,)),
     ]
-    return pl.pallas_call(
+    new_gate, new_up, hidden = pl.pallas_call(
         kernel,
         out_shape=(
-            jax.ShapeDtypeStruct((DEPTH, FF), BF),
-            jax.ShapeDtypeStruct((DEPTH, FF), BF),
-            jax.ShapeDtypeStruct((ROWS, FF), BF),
+            pltpu.VMEM((FF, DEPTH), BF),
+            pltpu.VMEM((FF, DEPTH), BF),
+            pltpu.VMEM((ROWS, FF), BF),
         ),
         in_specs=[vmem, anywhere, anywhere, vmem, vmem, vmem, vmem, smem, smem],
-        out_specs=(anywhere, anywhere, vmem),
+        out_specs=(vmem, vmem, vmem),
         scratch_shapes=scratch,
         compiler_params=pltpu.CompilerParams(
             collective_id=0, has_side_effects=True, vmem_limit_bytes=56 * 1024 * 1024
         ),
         cost_estimate=pl.CostEstimate(flops=7_000_000_000, bytes_accessed=10_000_000, transcendentals=200_000),
     )(*args)
+    return new_gate.T, new_up.T, hidden
 
 
 def solution(mesh):

time: 111 us -> 92.4 us (0.83)
  local copies, waits for them, and re-layouts: 16.9 us -> 3.23 us
  Pallas kernels: 92.1 us -> 87.1 us
    unnamed x11 -> x3, local copies, waits for them, and re-layouts: 10.5 us -> 3.23 us
    pallas_call x2 -> x0, local copies, waits for them, and re-layouts: 6.37 us -> none  [body(): pl.pallas_call(kernel, out_shape=(jax.ShapeDtypeStruct((DEPTH, FF), BF),...]
    pallas_call x1, Pallas kernels: 92.1 us -> 87.1 us  [body(): pl.pallas_call(kernel, out_shape=(pltpu.VMEM((FF, DEPTH), BF), pltpu.VMEM...]
where the time goes in v2:
time: 92.4 us; the launch traced here: 92.3 us
  Pallas kernels  87.1 us (94%)
  local copies, waits for them, and re-layouts  3.23 us (3%)
  between operations  1.93 us (2%)
    pallas_call x1, Pallas kernels, body(): pl.pallas_call(kernel, out_shape=(pltpu.VMEM((FF, DEPTH), BF), pltpu.VMEM...  87.1 us
    unnamed x3, local copies, waits for them, and re-layouts  3.23 us

profile of v2, /device:TPU:16, one launch (start us, length us, event | category | flops | bytes accessed | tf_op | source)
XLA Modules:
  0.0 92.3 jit_solution(17418171333220221000)
XLA Ops:
  1.9 87.1 %shard_map.112 = (bf16[1848,512]{1,0:T(8,128)(2,1)S(1)}, bf16[1848,512]{1,0:T(8,128)(2,1)S(1)}, bf16[96,1848]{1,0:T(8,128)(2,1)S(1)}) custom-call(bf16[96,512]{1,0:T(8,128)(2,1)} %tok.1, bf16[1848,512]{1,0:T(8,128)(2,1)} %bitcast.8, bf16[1848,512]{1,0:T(8,128)(2,1)} %bitcast.9, bf16[1,64,512]{2,1,0:T(8,128)(2,1)} %bitcast.10, bf16[1,64,512]{2,1,0:T(8,128)(2,1)} %bitcast.11, ...), custom_call_target="tpu_custom_call" | custom-call | flops 7000000000 | bytes 10000000 | tf_op jit(solution)/shard_map/pallas_call | solution.py:467
  89.1 1.2 %copy.15 = bf16[512,1848]{0,1:T(8,128)(2,1)} copy(bf16[512,1848]{0,1:T(8,128)(2,1)S(1)} %bitcast.7) | data formatting | bytes 3784704
  90.3 1.2 %copy.16 = bf16[512,1848]{0,1:T(8,128)(2,1)} copy(bf16[512,1848]{0,1:T(8,128)(2,1)S(1)} %bitcast.6) | data formatting | bytes 3784704
  91.6 0.7 copy.17

commit v3 on v2

--- a/solution.py
+++ b/solution.py
@@ -11,8 +11,8 @@
 WIDE, CHUNKS = 256, 7
 MAIN = WIDE * CHUNKS
 LAST = FF - MAIN
-CROSS = (0, 2, 4)
-ALONG = (1, 3, 5, 6)
+CROSS = (1, 3, 5)
+ALONG = (0, 2, 4, 6)
 
 
 class Semaphores:
@@ -24,9 +24,9 @@
 
 
 def kernel(
-    tok, gw, uw, gl, ul, gu, uu, out_s, inc_s,
+    tok_in, gw, uw, gl_in, ul_in, gu_in, uu_in, out_s, inc_s,
     vg, vu, hid,
-    T, wg, wu, wc, wt, lc, l0, ls, lr, lf, uc, u0, us, ur, uf,
+    tok, gl, ul, gu, uu, T, wg, wu, wc, wt, lc, l0, ls, lr, lf, uc, u0, us, ur, uq, ux, uf,
     part, parts_last, rx, qo, qa, ro, ra, acc, fs, fx, to, ta, tacc, ts, tx,
     ssem, rsem, lsem,
 ):
@@ -43,8 +43,12 @@
     up_y = (yp * 4 + xm * 2 + k, col)
     down_y = (ym * 4 + xm * 2 + k, col)
     far_x = (row, (1 - xh) * 8 + z)
+    far_partner = (chip * 2 + 1 - k, (1 - xh) * 8 + z)
     up_z = (row, xh * 8 + (z + 1) % 8)
     down_z = (row, xh * 8 + (z + 7) % 8)
+
+    def ring_y(i):
+        return ((y + i) % 4 * 4 + xm * 2 + k, col)
 
     def copy(src, dst, target, index):
         return pltpu.make_async_remote_copy(
@@ -60,18 +64,29 @@
         sent.append(c)
         return c
 
+    barrier = pltpu.get_barrier_semaphore()
+    pl.semaphore_signal(barrier, inc=1, device_id=partner, device_id_type=MESH)
+    pl.semaphore_signal(barrier, inc=1, device_id=far_x, device_id_type=MESH)
+    pl.semaphore_signal(barrier, inc=1, device_id=far_partner, device_id_type=MESH)
+    pl.semaphore_signal(barrier, inc=1, device_id=cross, device_id_type=MESH)
+    for i in range(1, 4):
+        pl.semaphore_signal(barrier, inc=1, device_id=ring_y(i), device_id_type=MESH)
+    for i in range(1, 8):
+        pl.semaphore_signal(barrier, inc=1, device_id=(row, xh * 8 + (z + i) % 8), device_id_type=MESH)
+
+    loads = [
+        pltpu.make_async_copy(src, dst, lsem.at[2 + i])
+        for i, (src, dst) in enumerate(((gu_in, gu), (uu_in, uu), (gl_in, gl), (ul_in, ul), (tok_in, tok)))
+    ]
+    for c in loads:
+        c.start()
     load_g = pltpu.make_async_copy(gw, wg, lsem.at[0])
     load_u = pltpu.make_async_copy(uw, wu, lsem.at[1])
     load_g.start()
     load_u.start()
 
-    barrier = pltpu.get_barrier_semaphore()
-    pl.semaphore_signal(barrier, inc=1, device_id=partner, device_id_type=MESH)
-    pl.semaphore_signal(barrier, inc=1, device_id=far_x, device_id_type=MESH)
-    for i in range(1, 8):
-        pl.semaphore_signal(barrier, inc=1, device_id=((chip + i) % 8 * 2 + k, col), device_id_type=MESH)
-        pl.semaphore_signal(barrier, inc=1, device_id=(row, xh * 8 + (z + i) % 8), device_id_type=MESH)
-
+    for c in loads:
+        c.wait()
     new, old = inc_s[0], out_s[0]
     for m, ref in enumerate((gu, uu)):
         b = ref[0]
@@ -81,7 +96,7 @@
         a = ref[0]
         lc[8 * m:8 * m + 4] = jnp.where(new == col, a, jnp.zeros_like(a)).reshape(4, 16, DEPTH)
         lc[8 * m + 4:8 * m + 8] = jnp.where(old == col, a, jnp.zeros_like(a)).reshape(4, 16, DEPTH)
-    pl.semaphore_wait(barrier, 16)
+    pl.semaphore_wait(barrier, 14)
 
     even = k == z % 2
     odd = jnp.logical_not(even)
@@ -91,17 +106,27 @@
         for p in range(PARTS)
     ]
 
+
+    def far(p, half, place):
+        rows = slice(PART * p, PART * (p + 1))
+        dst = T.at[xs, place, rows, DEPTH * half:DEPTH * (half + 1)]
+        return copy(tok.at[rows], dst, (far_x, far_partner)[half], names.of("h", p, half))
+
     @pl.when(odd)
     def _():
-        for c in t0:
-            c.start()
+        for p in range(PARTS):
+            t0[p].start()
+        for p in range(PARTS):
+            far(p, 1, ys).start()
 
     @pl.when(even)
     def _():
+        for p in range(PARTS):
+            far(p, 0, ys).start()
         T[xs, ys, :, 0:DEPTH] = tok[...]
 
+    c_u0 = send(uc.at[1 - k], u0, partner, "u0")
     c_l0 = send(lc.at[pl.ds(8 * (1 - xh), 8)], l0, far_x, "l0")
-    c_u0 = send(uc.at[1 - k], u0, partner, "u0")
 
     def block(zz, q, p):
         return T.at[(zz // 2) % 2, (xh + q) % 2 * 2 + zz // 4, PART * p:PART * (p + 1)]
@@ -113,9 +138,6 @@
     def source(direction, distance):
         return (z - distance + 8) % 8 if direction == 0 else (z + distance) % 8
 
-    def far(p, q):
-        return copy(block(z, q, p), block(z, q, p), far_x, names.of("h", p))
-
     def forward(stage, q):
         for p in range(PARTS):
             for d in range(2):
@@ -129,11 +151,10 @@
             t0[p].wait_recv()
             for d in range(2):
                 hop(d, 1, 0, p, z).start()
-            far(p, 0).start()
 
     c_u0.wait_recv()
     us[...] = uc[k] + u0[...]
-    u1 = [send(us.at[(chip + i) % 8], ur.at[i - 1], ((chip + i) % 8 * 2 + k, col), "u1", i) for i in range(1, 8)]
+    u1 = [send(us.at[pl.ds((y + i) % 4 * 2, 2)], ur.at[i - 1], ring_y(i), "u1", i) for i in range(1, 4)]
 
     @pl.when(odd)
     def _():
@@ -146,7 +167,8 @@
     @pl.when(even)
     def _():
         for p in range(PARTS):
-            far(p, 1).wait_recv()
+            for half in range(2):
+                far(p, half, (ys + 2) % 4).wait_recv()
             for d in range(2):
                 hop(d, 1, 1, p, z).start()
         forward(2, 0)
@@ -154,6 +176,14 @@
     @pl.when(odd)
     def _():
         forward(1, 1)
+
+    for c in u1:
+        c.wait_recv()
+    total = us[pl.ds(2 * y, 2)].astype(F32)
+    for i in range(3):
+        total = total + ur[i].astype(F32)
+    uq[...] = total.astype(BF)
+    c_ux = send(uq.at[xo], ux, cross, "ux")
 
     for c in l1:
         c.wait_recv()
@@ -165,18 +195,20 @@
     l2 = [send(lf.at[mine], lf.at[mine], (row, xh * 8 + (z + i) % 8), "l2", i) for i in range(1, 8)]
     l3 = [send(lf.at[mine], lf.at[mine], far_x, "l3", 0)]
 
-    for c in u1:
-        c.wait_recv()
-    total = us[chip].astype(F32)
-    for i in range(7):
-        total = total + ur[i].astype(F32)
-    uf[k, chip] = total.astype(BF)
-    u2 = [send(uf.at[k, chip], uf.at[k, chip], ((chip + i) % 8 * 2 + k, col), "u2", i) for i in range(1, 8)]
+    c_ux.wait_recv()
+    uf[k, chip] = uq[xm] + ux[...]
+    c_ua = send(uf.at[k, chip], uf.at[k, chip], cross, "ua")
+    u2 = [send(uf.at[k, chip], uf.at[k, chip], ring_y(i), "u2", i) for i in range(1, 4)]
     u3 = [send(uf.at[k, chip], uf.at[k, chip], partner, "u3", 0)]
 
     @pl.when(odd)
     def _():
         forward(3, 0)
+
+    beside = 2 * y + xo
+    c_ua.wait_recv()
+    u2b = [send(uf.at[k, beside], uf.at[k, beside], ring_y(i), "u2b", i) for i in range(1, 4)]
+    u3.append(send(uf.at[k, beside], uf.at[k, beside], partner, "u3", 4))
 
     @pl.when(even)
     def _():
@@ -191,10 +223,14 @@
     def _():
         forward(3, 1)
 
-    for i in range(1, 8):
+    for i in range(1, 4):
         u2[i - 1].wait_recv()
-        s = (chip - i + 8) % 8
+        s = (y - i + 4) % 4 * 2 + xm
         u3.append(send(uf.at[k, s], uf.at[k, s], partner, "u3", i))
+    for i in range(1, 4):
+        u2b[i - 1].wait_recv()
+        s = (y - i + 4) % 4 * 2 + xo
+        u3.append(send(uf.at[k, s], uf.at[k, s], partner, "u3", 4 + i))
 
     for c in l3:
         c.wait_recv()
@@ -227,13 +263,16 @@
         swap(j).start()
         return carry
 
-    lax.fori_loop(0, CHUNKS, merge, 0)
-    wt[:, 0:DEPTH] = jnp.zeros((128, DEPTH), BF)
-    for m, (w, v) in enumerate(((wg, vg), (wu, vu))):
-        piece = merged(w, m, slice(MAIN, FF))
-        v[MAIN:FF] = piece
-        wt[64 * m:64 * m + LAST, 0:DEPTH] = piece
-    c_wt = send(wt.at[:, 0:DEPTH], wt.at[:, DEPTH:], partner, "wt")
+    def merge_last():
+        wt[:, 0:DEPTH] = jnp.zeros((128, DEPTH), BF)
+        for m, (w, v) in enumerate(((wg, vg), (wu, vu))):
+            piece = merged(w, m, slice(MAIN, FF))
+            v[MAIN:FF] = piece
+            wt[64 * m:64 * m + LAST, 0:DEPTH] = piece
+        return send(wt.at[:, 0:DEPTH], wt.at[:, DEPTH:], partner, "wt")
+
+    lax.fori_loop(0, AHEAD, merge, 0)
+
     @pl.when(even)
     def _():
         for p in range(PARTS):
@@ -256,7 +295,7 @@
 
         lax.fori_loop(0, 4, quarter, 0)
 
-    def compute_last():
+    def compute_last(c_wt):
         c_wt.wait_recv()
         for x in range(2):
             p = times(x, wt[...])
@@ -375,7 +414,11 @@
     for j in range(CHUNKS):
         compute(j)
         (crossed[CROSS.index(j)] if j in CROSS else along[ALONG.index(j)]).start()
-    compute_last()
+        if j + AHEAD < CHUNKS:
+            merge(j + AHEAD, 0)
+        elif j + AHEAD == CHUNKS:
+            c_wt = merge_last()
+    compute_last(c_wt)
     last.start()
     along[0].forward()
     along[1].forward()
@@ -410,7 +453,7 @@
     @pl.when(even)
     def _():
         for p in range(PARTS):
-            far(p, 0).wait_send()
+            far(p, 0, ys).wait_send()
             for q in range(2):
                 for d in range(2):
                     hop(d, 1, q, p, z).wait_send()
@@ -420,6 +463,7 @@
     def _():
         for p in range(PARTS):
             t0[p].wait_send()
+            far(p, 1, ys).wait_send()
             for q in range(2):
                 for d in range(2):
                     hop(d, 2, q, p, source(d, 1)).wait_send()
@@ -429,8 +473,19 @@
     assert len(names.names) <= COPIES, len(names.names)
 
 
+def store(a, b, c, x, y, z, sems):
+    copies = [
+        pltpu.make_async_copy(src, dst, sems.at[i]) for i, (src, dst) in enumerate(((a, x), (b, y), (c, z)))
+    ]
+    for c in copies:
+        c.start()
+    for c in copies:
+        c.wait()
+
+
 COPIES = 192
 PARTS = 3
+AHEAD = 2
 PART = ROWS // PARTS
 
 
@@ -450,19 +505,20 @@
         return pltpu.VMEM(shape, F32)
 
     scratch = [
+        b(ROWS, DEPTH), b(1, RANK, DEPTH), b(1, RANK, DEPTH), b(1, RANK, FF), b(1, RANK, FF),
         b(2, 4, ROWS, 2 * DEPTH),
         b(FF, DEPTH), b(FF, DEPTH),
         b(CHUNKS, 2, WIDE, 2 * DEPTH),
         b(128, 2 * DEPTH),
         b(16, 16, DEPTH), b(8, 16, DEPTH), b(8, 16, DEPTH), b(7, 16, DEPTH), b(16, 16, DEPTH),
-        b(2, 8, 16, FF), b(8, 16, FF), b(8, 16, FF), b(7, 16, FF), b(2, 8, 16, FF),
+        b(2, 8, 16, FF), b(8, 16, FF), b(8, 16, FF), b(3, 2, 16, FF), b(2, 16, FF), b(16, FF), b(2, 8, 16, FF),
         b(CHUNKS, 2, 2, 4, ROWS, WIDE),
         b(2, 4, ROWS, 128),
         b(n_c, 2, 4, ROWS, WIDE), b(n_c, 2, ROWS, WIDE), b(n_c, 2, 2, ROWS, WIDE),
         b(n_a, 2, 2, ROWS, WIDE), b(n_a, 2, 2, 2, ROWS, WIDE),
         f(n_a, 2, ROWS, WIDE), b(n_a, 2, ROWS, WIDE), b(n_a, 2, ROWS, WIDE),
         b(2, ROWS, 128), b(2, 2, ROWS, 128), f(ROWS, 128), b(ROWS, 128), b(ROWS, 128),
-        pltpu.SemaphoreType.DMA((COPIES,)), pltpu.SemaphoreType.DMA((COPIES,)), pltpu.SemaphoreType.DMA((4,)),
+        pltpu.SemaphoreType.DMA((COPIES,)), pltpu.SemaphoreType.DMA((COPIES,)), pltpu.SemaphoreType.DMA((7,)),
     ]
     new_gate, new_up, hidden = pl.pallas_call(
         kernel,
@@ -471,7 +527,7 @@
             pltpu.VMEM((FF, DEPTH), BF),
             pltpu.VMEM((ROWS, FF), BF),
         ),
-        in_specs=[vmem, anywhere, anywhere, vmem, vmem, vmem, vmem, smem, smem],
+        in_specs=[anywhere] * 7 + [smem] * 2,
         out_specs=(vmem, vmem, vmem),
         scratch_shapes=scratch,
         compiler_params=pltpu.CompilerParams(
@@ -479,6 +535,18 @@
         ),
         cost_estimate=pl.CostEstimate(flops=7_000_000_000, bytes_accessed=10_000_000, transcendentals=200_000),
     )(*args)
+    new_gate, new_up, hidden = pl.pallas_call(
+        store,
+        out_shape=(
+            jax.ShapeDtypeStruct((FF, DEPTH), BF),
+            jax.ShapeDtypeStruct((FF, DEPTH), BF),
+            jax.ShapeDtypeStruct((ROWS, FF), BF),
+        ),
+        in_specs=[anywhere] * 3,
+        out_specs=(anywhere,) * 3,
+        scratch_shapes=[pltpu.SemaphoreType.DMA((3,))],
+        compiler_params=pltpu.CompilerParams(vmem_limit_bytes=1024 * 1024),
+    )(new_gate, new_up, hidden)
     return new_gate.T, new_up.T, hidden
 
 

time: 92.4 us -> 88.5 us (0.958)
  local copies, waits for them, and re-layouts: 3.23 us -> 0 us
    unnamed x3 -> x0, local copies, waits for them, and re-layouts: 3.23 us -> none
    pallas_call x1, Pallas kernels: 87.1 us -> 84.5 us  [body(): pl.pallas_call(kernel, out_shape=(pltpu.VMEM((FF, DEPTH), BF), pltpu.VMEM...]
    pallas_call x0 -> x1, Pallas kernels: none -> 2.01 us  [body(): pl.pallas_call(store, out_shape=(jax.ShapeDtypeStruct((FF, DEPTH), BF), j...]
where the time goes in v3:
time: 88.5 us; the launch traced here: 88.4 us
  Pallas kernels  86.5 us (98%)
  between operations  1.93 us (2%)
    pallas_call x1, Pallas kernels, body(): pl.pallas_call(kernel, out_shape=(pltpu.VMEM((FF, DEPTH), BF), pltpu.VMEM...  84.5 us
    pallas_call x1, Pallas kernels, body(): pl.pallas_call(store, out_shape=(jax.ShapeDtypeStruct((FF, DEPTH), BF), j...  2.01 us

profile of v3, /device:TPU:16, one launch (start us, length us, event | category | flops | bytes accessed | tf_op | source)
XLA Modules:
  0.0 88.4 jit_solution(2815991021570819241)
XLA Ops:
  1.9 84.5 %shard_map.112 = (bf16[1848,512]{1,0:T(8,128)(2,1)S(1)}, bf16[1848,512]{1,0:T(8,128)(2,1)S(1)}, bf16[96,1848]{1,0:T(8,128)(2,1)S(1)}) custom-call(bf16[96,512]{1,0:T(8,128)(2,1)} %tok_in.1, bf16[1848,512]{1,0:T(8,128)(2,1)} %bitcast.6, bf16[1848,512]{1,0:T(8,128)(2,1)} %bitcast.7, bf16[1,64,512]{2,1,0:T(8,128)(2,1)} %bitcast.10, ...), custom_call_target="tpu_custom_call" | custom-call | flops 7000000000 | bytes 10000000 | tf_op jit(solution)/shard_map/pallas_call | solution.py:523
  86.4 2.0 %shard_map.113 = (bf16[1848,512]{1,0:T(8,128)(2,1)}, bf16[1848,512]{1,0:T(8,128)(2,1)}, bf16[96,1848]{1,0:T(8,128)(2,1)}) custom-call(bf16[1848,512]{1,0:T(8,128)(2,1)S(1)} %get-tuple-element.9.a, bf16[1848,512]{1,0:T(8,128)(2,1)S(1)} %get-tuple-element.10.b, bf16[96,1848]{1,0:T(8,128)(2,1)S(1)} %get-tuple-element.11.c), custom_call_target="tpu_custom_call" | custom-call | tf_op jit(solution)/shard_map/pallas_call | solution.py:538

commit v4 on v3

--- a/solution.py
+++ b/solution.py
@@ -271,6 +271,7 @@
             wt[64 * m:64 * m + LAST, 0:DEPTH] = piece
         return send(wt.at[:, 0:DEPTH], wt.at[:, DEPTH:], partner, "wt")
 
+    c_wt = merge_last()
     lax.fori_loop(0, AHEAD, merge, 0)
 
     @pl.when(even)
@@ -284,16 +285,17 @@
             T[x].reshape(4 * ROWS, 2 * DEPTH), w, (((1,), (1,)), ((), ())), preferred_element_type=F32
         )
 
-    def compute(j):
+    def compute(j, unit=None):
         swap(j).wait_recv()
 
-        def quarter(i, carry):
-            m, x = i // 2, i % 2
-            p = times(x, wc[j, m])
-            part[j, m, x] = p.astype(BF).reshape(4, ROWS, WIDE)
-            return carry
-
-        lax.fori_loop(0, 4, quarter, 0)
+        for m in range(2):
+            def half(x, carry):
+                part[j, m, x] = times(x, wc[j, m]).astype(BF).reshape(4, ROWS, WIDE)
+                return carry
+
+            lax.fori_loop(0, 2, half, 0)
+            if unit is not None:
+                unit.start(m)
 
     def compute_last(c_wt):
         c_wt.wait_recv()
@@ -314,11 +316,12 @@
     class Along:
         def __init__(self, i, j):
             self.i, self.j = i, j
-
-        def start(self):
-            i, j = self.i, self.j
-            self.opposite = [send(part.at[j, d, :, yo], ro.at[i, d], ways[d], "ro", i, d) for d in range(2)]
-            self.arrive = [send(part.at[j, 1 - d, :, near[d]], ra.at[i, d, 1 - d], ways[d], "ra", i, d, 1 - d) for d in range(2)]
+            self.opposite, self.arrive, self.first = [], [], []
+
+        def start(self, m):
+            i, j = self.i, self.j
+            self.opposite.append(send(part.at[j, m, :, yo], ro.at[i, m], ways[m], "ro", i, m))
+            self.arrive.append(send(part.at[j, m, :, near[1 - m]], ra.at[i, 1 - m, m], ways[1 - m], "ra", i, 1 - m, m))
 
         def forward(self):
             i, j = self.i, self.j
@@ -349,15 +352,16 @@
     class Cross:
         def __init__(self, i, j):
             self.i, self.j = i, j
-
-        def start(self):
-            i, j = self.i, self.j
-            self.first = send(part.at[j, :, xo], rx.at[i], cross, "rx", i)
+            self.opposite, self.arrive, self.first = [], [], []
+
+        def start(self, m):
+            i, j = self.i, self.j
+            self.first.append(send(part.at[j, m, xo], rx.at[i, m], cross, "rx", i, m))
 
         def turn(self):
             i, j = self.i, self.j
-            self.first.wait_recv()
             for m in range(2):
+                self.first[m].wait_recv()
                 add(part.at[j, m, xm], rx.at[i, m])
             self.opposite = [send(part.at[j, d, xm, yo], qo.at[i, d], ways[d], "qo", i, d) for d in range(2)]
             self.arrive = [send(part.at[j, 1 - d, xm, near[d]], qa.at[i, d, 1 - d], ways[d], "qa", i, d, 1 - d) for d in range(2)]
@@ -411,15 +415,12 @@
     along = [Along(i, j) for i, j in enumerate(ALONG)]
     crossed = [Cross(i, j) for i, j in enumerate(CROSS)]
     last = Last()
+    compute_last(c_wt)
+    last.start()
     for j in range(CHUNKS):
-        compute(j)
-        (crossed[CROSS.index(j)] if j in CROSS else along[ALONG.index(j)]).start()
+        compute(j, crossed[CROSS.index(j)] if j in CROSS else along[ALONG.index(j)])
         if j + AHEAD < CHUNKS:
             merge(j + AHEAD, 0)
-        elif j + AHEAD == CHUNKS:
-            c_wt = merge_last()
-    compute_last(c_wt)
-    last.start()
     along[0].forward()
     along[1].forward()
     crossed[0].turn()

time: 88.5 us -> 87.3 us (0.986)
  Pallas kernels: 86.5 us -> 85.3 us
    pallas_call x1, Pallas kernels: 84.5 us -> 83.2 us  [body(): pl.pallas_call(kernel, out_shape=(pltpu.VMEM((FF, DEPTH), BF), pltpu.VMEM...]
where the time goes in v4:
time: 87.3 us; the launch traced here: 87.2 us
  Pallas kernels  85.3 us (98%)
  between operations  1.93 us (2%)
    pallas_call x1, Pallas kernels, body(): pl.pallas_call(kernel, out_shape=(pltpu.VMEM((FF, DEPTH), BF), pltpu.VMEM...  83.2 us
    pallas_call x1, Pallas kernels, body(): pl.pallas_call(store, out_shape=(jax.ShapeDtypeStruct((FF, DEPTH), BF), j...  2.01 us

profile of v4, /device:TPU:16, one launch (start us, length us, event | category | flops | bytes accessed | tf_op | source)
XLA Modules:
  0.0 87.2 jit_solution(1361664987292182308)
XLA Ops:
  1.9 83.2 %shard_map.112 = (bf16[1848,512]{1,0:T(8,128)(2,1)S(1)}, bf16[1848,512]{1,0:T(8,128)(2,1)S(1)}, bf16[96,1848]{1,0:T(8,128)(2,1)S(1)}) custom-call(bf16[96,512]{1,0:T(8,128)(2,1)} %tok_in.1, bf16[1848,512]{1,0:T(8,128)(2,1)} %bitcast.6, bf16[1848,512]{1,0:T(8,128)(2,1)} %bitcast.7, bf16[1,64,512]{2,1,0:T(8,128)(2,1)} %bitcast.10, ...), custom_call_target="tpu_custom_call" | custom-call | flops 7000000000 | bytes 10000000 | tf_op jit(solution)/shard_map/pallas_call | solution.py:524
  85.2 2.0 %shard_map.113 = (bf16[1848,512]{1,0:T(8,128)(2,1)}, bf16[1848,512]{1,0:T(8,128)(2,1)}, bf16[96,1848]{1,0:T(8,128)(2,1)}) custom-call(bf16[1848,512]{1,0:T(8,128)(2,1)S(1)} %get-tuple-element.9.a, bf16[1848,512]{1,0:T(8,128)(2,1)S(1)} %get-tuple-element.10.b, bf16[96,1848]{1,0:T(8,128)(2,1)S(1)} %get-tuple-element.11.c), custom_call_target="tpu_custom_call" | custom-call | tf_op jit(solution)/shard_map/pallas_call | solution.py:539

commit v5 on v4

--- a/solution.py
+++ b/solution.py
@@ -272,7 +272,7 @@
         return send(wt.at[:, 0:DEPTH], wt.at[:, DEPTH:], partner, "wt")
 
     c_wt = merge_last()
-    lax.fori_loop(0, AHEAD, merge, 0)
+    merge(0, 0)
 
     @pl.when(even)
     def _():
@@ -415,8 +415,11 @@
     along = [Along(i, j) for i, j in enumerate(ALONG)]
     crossed = [Cross(i, j) for i, j in enumerate(CROSS)]
     last = Last()
+    waited = len(sent)
     compute_last(c_wt)
     last.start()
+    for j in range(1, AHEAD):
+        merge(j, 0)
     for j in range(CHUNKS):
         compute(j, crossed[CROSS.index(j)] if j in CROSS else along[ALONG.index(j)])
         if j + AHEAD < CHUNKS:
@@ -434,6 +437,31 @@
     crossed[1].forward()
     along[2].gather()
     crossed[0].end()
+    for c in sent[:waited]:
+        c.wait_send()
+    for j in range(CHUNKS):
+        swap(j).wait_send()
+
+    @pl.when(even)
+    def _():
+        for p in range(PARTS):
+            far(p, 0, ys).wait_send()
+            for q in range(2):
+                for d in range(2):
+                    hop(d, 1, q, p, z).wait_send()
+                    hop(d, 3, q, p, source(d, 2)).wait_send()
+
+    @pl.when(odd)
+    def _():
+        for p in range(PARTS):
+            t0[p].wait_send()
+            far(p, 1, ys).wait_send()
+            for q in range(2):
+                for d in range(2):
+                    hop(d, 2, q, p, source(d, 1)).wait_send()
+                    if d == q:
+                        hop(d, 4, q, p, source(d, 3)).wait_send()
+
     crossed[2].turn()
     along[3].gather()
     last.gather()
@@ -446,31 +474,8 @@
     last.end()
     crossed[2].end()
 
-    for c in sent:
+    for c in sent[waited:]:
         c.wait_send()
-    for j in range(CHUNKS):
-        swap(j).wait_send()
-
-    @pl.when(even)
-    def _():
-        for p in range(PARTS):
-            far(p, 0, ys).wait_send()
-            for q in range(2):
-                for d in range(2):
-                    hop(d, 1, q, p, z).wait_send()
-                    hop(d, 3, q, p, source(d, 2)).wait_send()
-
-    @pl.when(odd)
-    def _():
-        for p in range(PARTS):
-            t0[p].wait_send()
-            far(p, 1, ys).wait_send()
-            for q in range(2):
-                for d in range(2):
-                    hop(d, 2, q, p, source(d, 1)).wait_send()
-                    if d == q:
-                        hop(d, 4, q, p, source(d, 3)).wait_send()
-
     assert len(names.names) <= COPIES, len(names.names)
 
 

time: 87.3 us -> 87.2 us (level)
  no operation moved by 1% of the time
where the time goes in v5:
time: 87.2 us; the launch traced here: 87.1 us
  Pallas kernels  85.2 us (98%)
  between operations  1.93 us (2%)
    pallas_call x1, Pallas kernels, body(): pl.pallas_call(kernel, out_shape=(pltpu.VMEM((FF, DEPTH), BF), pltpu.VMEM...  83.1 us
    pallas_call x1, Pallas kernels, body(): pl.pallas_call(store, out_shape=(jax.ShapeDtypeStruct((FF, DEPTH), BF), j...  2.01 us

profile of v5, /device:TPU:16, one launch (start us, length us, event | category | flops | bytes accessed | tf_op | source)
XLA Modules:
  0.0 87.1 jit_solution(4111769864123783985)
XLA Ops:
  1.9 83.1 %shard_map.112 = (bf16[1848,512]{1,0:T(8,128)(2,1)S(1)}, bf16[1848,512]{1,0:T(8,128)(2,1)S(1)}, bf16[96,1848]{1,0:T(8,128)(2,1)S(1)}) custom-call(bf16[96,512]{1,0:T(8,128)(2,1)} %tok_in.1, bf16[1848,512]{1,0:T(8,128)(2,1)} %bitcast.6, bf16[1848,512]{1,0:T(8,128)(2,1)} %bitcast.7, bf16[1,64,512]{2,1,0:T(8,128)(2,1)} %bitcast.10, ...), custom_call_target="tpu_custom_call" | custom-call | flops 7000000000 | bytes 10000000 | tf_op jit(solution)/shard_map/pallas_call | solution.py:529
  85.1 2.0 %shard_map.113 = (bf16[1848,512]{1,0:T(8,128)(2,1)}, bf16[1848,512]{1,0:T(8,128)(2,1)}, bf16[96,1848]{1,0:T(8,128)(2,1)}) custom-call(bf16[1848,512]{1,0:T(8,128)(2,1)S(1)} %get-tuple-element.9.a, bf16[1848,512]{1,0:T(8,128)(2,1)S(1)} %get-tuple-element.10.b, bf16[96,1848]{1,0:T(8,128)(2,1)S(1)} %get-tuple-element.11.c), custom_call_target="tpu_custom_call" | custom-call | tf_op jit(solution)/shard_map/pallas_call | solution.py:544

commit v6 on v5

--- a/solution.py
+++ b/solution.py
@@ -490,7 +490,7 @@
 
 
 COPIES = 192
-PARTS = 3
+PARTS = 2
 AHEAD = 2
 PART = ROWS // PARTS
 

time: 87.2 us -> 86.9 us (level)
  no operation moved by 1% of the time
where the time goes in v6:
time: 86.9 us; the launch traced here: 86.8 us
  Pallas kernels  84.9 us (98%)
  between operations  1.93 us (2%)
    pallas_call x1, Pallas kernels, body(): pl.pallas_call(kernel, out_shape=(pltpu.VMEM((FF, DEPTH), BF), pltpu.VMEM...  82.9 us
    pallas_call x1, Pallas kernels, body(): pl.pallas_call(store, out_shape=(jax.ShapeDtypeStruct((FF, DEPTH), BF), j...  2.01 us

profile of v6, /device:TPU:16, one launch (start us, length us, event | category | flops | bytes accessed | tf_op | source)
XLA Modules:
  0.0 86.8 jit_solution(281866618400627701)
XLA Ops:
  1.9 82.9 %shard_map.112 = (bf16[1848,512]{1,0:T(8,128)(2,1)S(1)}, bf16[1848,512]{1,0:T(8,128)(2,1)S(1)}, bf16[96,1848]{1,0:T(8,128)(2,1)S(1)}) custom-call(bf16[96,512]{1,0:T(8,128)(2,1)} %tok_in.1, bf16[1848,512]{1,0:T(8,128)(2,1)} %bitcast.6, bf16[1848,512]{1,0:T(8,128)(2,1)} %bitcast.7, bf16[1,64,512]{2,1,0:T(8,128)(2,1)} %bitcast.10, ...), custom_call_target="tpu_custom_call" | custom-call | flops 7000000000 | bytes 10000000 | tf_op jit(solution)/shard_map/pallas_call | solution.py:529
  84.8 2.0 %shard_map.113 = (bf16[1848,512]{1,0:T(8,128)(2,1)}, bf16[1848,512]{1,0:T(8,128)(2,1)}, bf16[96,1848]{1,0:T(8,128)(2,1)}) custom-call(bf16[1848,512]{1,0:T(8,128)(2,1)S(1)} %get-tuple-element.9.a, bf16[1848,512]{1,0:T(8,128)(2,1)S(1)} %get-tuple-element.10.b, bf16[96,1848]{1,0:T(8,128)(2,1)S(1)} %get-tuple-element.11.c), custom_call_target="tpu_custom_call" | custom-call | tf_op jit(solution)/shard_map/pallas_call | solution.py:544
